TPU v7x, 32 devices: a whole 2x2x4 slice. The times are simulated.
32 devices in a mesh: groups: 2 (over y), inst: 4 (over x, core), tp: 4 (over z).
Axes of the slice: x: 2, y: 2, z: 4, core: 2. Of those that a mesh axis runs over, the one named last changes fastest.
Arguments:
- hidden: bfloat16 [2048, 5120], P(('groups', 'inst'), 'tp'), parts along dimension 0, may hold values from -6 to 6
- k_weight: bfloat16 [5120, 1024], P('inst', 'tp'), may hold values from -0.078125 to 0.078125
- v_weight: bfloat16 [5120, 1024], P('inst', 'tp'), may hold values from -0.078125 to 0.078125
- k_gain: float32 [128], replicated, may hold values from 0.25 to 1.75
- queries: bfloat16 [2048, 8192], P(('groups', 'inst'), 'tp'), parts along dimension 0, may hold values from -8 to 8
- kv_pool: bfloat16 [2, 432, 128, 1024], P(None, ('groups', 'inst'), None, 'tp'), parts along dimension 1, may hold values from -8 to 8
- page_holder: int32 [8, 48], P(('groups', 'inst')), parts along dimension 0, may hold values from 0 to 3, as said below
- page_slot: int32 [8, 48], P(('groups', 'inst')), parts along dimension 0, may hold values from 0 to 53, as said below
- page_count: int32 [8], P(('groups', 'inst')), parts along dimension 0, may hold values from 12 to 48, as said below
- write_owner: int32 [8, 2], P(('groups', 'inst')), parts along dimension 0, may hold values from 0 to 3, as said below
- write_slot: int32 [8, 2], P(('groups', 'inst')), parts along dimension 0, may hold values from 0 to 53, as said below
Outputs:
- attention_out: bfloat16 [2048, 8192], P(('groups', 'inst'), 'tp'), parts along dimension 0
- new_pool: bfloat16 [2, 432, 128, 1024], P(None, ('groups', 'inst'), None, 'tp'), parts along dimension 1
There are 2 independent parts, one for each index of `groups`. A program takes and returns all parts, laid end to end along the dimension named above; an argument that names none is the same for every part. Nothing has to cross between parts.
Inputs may be any that keep to these rules, and one draw needn't show every extreme that they name: `page_holder`: no request has more than 18 of its pages j < page_count on one instance; the request with 48 pages has exactly 18 on one instance. `page_slot`: the history pages in use and the new pages' slots are distinct slots of their instance. `page_count`: one request has exactly 48 pages. `write_owner`: the 2 new pages of one request go to distinct instances. `write_slot`: distinct from every slot in use on the same instance.
All inputs are finite; a program needn't handle non-finite values.
Results may differ from a plain program's by a relative error of at most 0.0039.
Values may be sent and summed in bfloat16 or wider, within the bound.
No kernel may reach another device: no remote copies, remote signals or barrier semaphores. Data moves between devices by JAX's collectives and lax.ppermute only.
A program may use at most 192 MiB of HBM per device.

v0:
```python
import functools
import math

import jax
import jax.numpy as jnp
from jax import lax
from jax.experimental import pallas as pl
from jax.experimental.pallas import tpu as pltpu
from jax.sharding import PartitionSpec as P

HD = 128
PAGE = 128
GROUP = 8
BLOCK = GROUP * HD
EXTRA = 128
TOTALS = 64
EMPTY = -1e30
LOG2E = 1.4426950408889634
SCALE = LOG2E / math.sqrt(HD)
CHUNK = 4
ANY = pl.BlockSpec(memory_space=pl.ANY)
SMEM = pl.BlockSpec(memory_space=pltpu.SMEM)
VMEM_LIMIT = 63 * 1024 * 1024


def cost(microseconds):
    return pl.CostEstimate(
        flops=int(microseconds * 1e9), bytes_accessed=int(microseconds * 3e6), transcendentals=0
    )


def row_dot(a, b):
    return lax.dot_general(a, b, (((1,), (1,)), ((), ())), preferred_element_type=jnp.float32)


def plain_dot(a, b):
    return lax.dot_general(a, b, (((1,), (0,)), ((), ())), preferred_element_type=jnp.float32)


def split_stats(stat, lane, lanes, terms):
    high = stat.astype(jnp.bfloat16).astype(jnp.float32)
    rest = stat - high
    middle = rest.astype(jnp.bfloat16).astype(jnp.float32)
    terms = jnp.where(lanes == lane, high, terms)
    terms = jnp.where(lanes == lane + 1, middle, terms)
    return jnp.where(lanes == lane + 2, rest - middle, terms)


def joined_stats(extra, lane):
    term = lax.broadcasted_iota(jnp.int32, (EXTRA, HD), 0)
    picked = jnp.where((term >= lane) & (term < lane + 3), 1.0, 0.0).astype(jnp.bfloat16)
    return plain_dot(extra, picked)


def state_stats(extra, head):
    return joined_stats(extra, 3 * head), joined_stats(extra, TOTALS + 3 * head)


def attend_kernel(plan, refs):
    requests, kv_heads, pages_listed = plan["requests"], plan["kv_heads"], plan["pages_listed"]
    copy_pool, resume = plan["copy_pool"], plan["resume"]
    width = len(kv_heads)
    items = requests * width
    refs = list(refs)
    me_ref, table_ref = refs.pop(0), refs.pop(0)
    q_refs = [refs.pop(0) for _ in range(requests)]
    state_ref = refs.pop(0) if resume else None
    pool_ref = refs.pop(0)
    out_refs = [refs.pop(0) for _ in range(items)]
    new_pool_ref = refs.pop(0) if copy_pool else None
    q_buf, kv_buf, acc, maxima, totals, slots, q_sem, kv_sem, out_sem = refs[:9]
    refs = refs[9:]
    if resume:
        send_buf = refs.pop(0)
    new_count = q_buf.shape[2]
    rows = GROUP * new_count
    shape = (GROUP, new_count, HD)
    lanes = lax.broadcasted_iota(jnp.int32, (new_count, HD), 1)

    def q_copies(item):
        offset = kv_heads[item % width] * BLOCK
        return [
            pltpu.make_async_copy(
                q_refs[item // width].at[:, pl.ds(offset + head * HD, HD)],
                q_buf.at[item, head],
                q_sem.at[item, head],
            )
            for head in range(GROUP)
        ]

    def page_copies(request, place, slot):
        return [
            pltpu.make_async_copy(
                pool_ref.at[:, slot, :, pl.ds(kv_head * HD, HD)],
                kv_buf.at[request, column, :, place],
                kv_sem.at[request, column, place],
            )
            for column, kv_head in enumerate(kv_heads)
        ]

    def out_copy(item, index):
        source, target = send_buf if resume else acc, out_refs[item]
        part = [pl.ds(0, GROUP), pl.ds(GROUP, 1)][index]
        return pltpu.make_async_copy(
            source.at[item, part], target.at[0, part], out_sem.at[item, index]
        )

    for item in range(items):
        for copy in q_copies(item):
            copy.start()
    if resume:
        state_copy = pltpu.make_async_copy(state_ref, acc, out_sem.at[0, 0])
        state_copy.start()
    me = me_ref[0]
    for request in range(requests):
        count = table_ref[request, 2 * pages_listed]

        def look(page, found, request=request, count=count):
            mine = (page < count) & (table_ref[request, page] == me)

            @pl.when(mine)
            def _():
                for copy in page_copies(request, found, table_ref[request, pages_listed + page]):
                    copy.start()

            return found + mine.astype(jnp.int32)

        slots[request] = lax.fori_loop(0, count, look, 0)
    pool_in, pool_out = [], []
    if copy_pool:
        pool_buf, pool_sem = refs
        slot_total = pool_ref.shape[1]
        parts = pool_sem.shape[1]
        step = slot_total // parts
        for index in range(2):
            for part in range(parts):
                piece = (index, pl.ds(part * step, step))
                sem = pool_sem.at[index, part]
                pool_in.append(pltpu.make_async_copy(pool_ref.at[piece], pool_buf.at[piece], sem))
                pool_out.append(
                    pltpu.make_async_copy(pool_buf.at[piece], new_pool_ref.at[piece], sem)
                )
        for copy in pool_in:
            copy.start()
    for item in range(items):
        for copy in q_copies(item):
            copy.wait()
    if resume:
        state_copy.wait()

    def one_item(item, carry):
        request = item // width
        column = item % width
        found = slots[request]
        sums = pl.ds(0, GROUP)
        if resume:
            extra = acc[item, GROUP].astype(jnp.bfloat16)
            for head in range(GROUP):
                maxima[head], total = state_stats(extra, head)
                totals[head] = jnp.where(lanes == 0, total, 0.0)
        else:
            acc[item, sums] = jnp.zeros(shape, jnp.float32)
            totals[...] = jnp.zeros(shape, jnp.float32)
            maxima[...] = jnp.full(shape, EMPTY, jnp.float32)

        @pl.when(column == 0)
        def _():
            def arrived(place, carry):
                for copy in page_copies(request, place, 0):
                    copy.wait()
                return carry

            lax.fori_loop(0, found, arrived, 0)

        def chunk(first, count):
            keys = kv_buf[request, column, 0, pl.ds(first, count)].reshape(count * PAGE, HD)
            values = kv_buf[request, column, 1, pl.ds(first, count)].reshape(count * PAGE, HD)
            scores = row_dot(q_buf[item].reshape(rows, HD), keys)
            old = maxima[...].reshape(rows, HD)
            top = jnp.maximum(old, jnp.max(scores, axis=1, keepdims=True) * SCALE)
            rescale = jnp.exp2(old - top)
            total = totals[...].reshape(rows, HD) * rescale
            pieces = []
            for part in range(count):
                piece = jnp.exp2(scores[:, part * PAGE : (part + 1) * PAGE] * SCALE - top)
                total = total + piece
                pieces.append(piece.astype(jnp.bfloat16))
            weights = jnp.concatenate(pieces, axis=1) if count > 1 else pieces[0]
            maxima[...] = top.reshape(shape)
            totals[...] = total.reshape(shape)
            acc[item, sums] = acc[item, sums] * rescale.reshape(shape) + plain_dot(
                weights, values
            ).reshape(shape)

        whole = found // CHUNK
        left = found % CHUNK

        def step(index, carry):
            chunk(index * CHUNK, CHUNK)
            return carry

        lax.fori_loop(0, whole, step, 0)
        for count in range(1, CHUNK):

            @pl.when(left == count)
            def _(count=count):
                chunk(whole * CHUNK, count)

        def send(index):
            for each in range(items):

                @pl.when(item == each)
                def _(each=each):
                    out_copy(each, index).start()

        if not resume:
            send(0)
        terms = jnp.zeros((new_count, HD), jnp.float32)
        for head in range(GROUP):
            total = jnp.sum(totals[head], axis=1, keepdims=True)
            if resume:
                some = total > 0.0
                safe = jnp.where(some, total, 1.0)
                send_buf[item, head] = (acc[item, head] * (1.0 / safe)).astype(jnp.bfloat16)
                stat = jnp.where(some, maxima[head] + jnp.log2(safe), EMPTY)
                terms = split_stats(stat, 3 * head, lanes, terms)
            else:
                terms = split_stats(maxima[head], 3 * head, lanes, terms)
                terms = split_stats(total, TOTALS + 3 * head, lanes, terms)
        if resume:
            send_buf[item, GROUP] = terms.astype(jnp.bfloat16)
            send(0)
        else:
            acc[item, GROUP] = terms
        send(1)
        if copy_pool:

            @pl.when(item == 0)
            def _():
                for copy_in, copy_out in zip(pool_in, pool_out):
                    copy_in.wait()
                    copy_out.start()

        return carry

    lax.fori_loop(0, items, one_item, 0)
    for item in range(items):
        for index in range(2):
            out_copy(item, index).wait()
    for copy in pool_out:
        copy.wait()


def attend(me, tables, asked, kv_heads, pool, pages_listed, capacity, state=None, copy_pool=False):
    requests, width, new_count = tables.shape[0], len(kv_heads), asked[0].shape[0]
    items = requests * width
    resume = state is not None
    blocks = (GROUP + 1, new_count, HD)
    kind = jnp.bfloat16 if resume else jnp.float32
    out_shape = [jax.ShapeDtypeStruct((1,) + blocks, kind) for _ in range(items)]
    scratch = [
        pltpu.VMEM((items, GROUP, new_count, HD), jnp.bfloat16),
        pltpu.VMEM((requests, width, 2, capacity, PAGE, HD), jnp.bfloat16),
        pltpu.VMEM((items,) + blocks, jnp.float32),
        pltpu.VMEM((GROUP, new_count, HD), jnp.float32),
        pltpu.VMEM((GROUP, new_count, HD), jnp.float32),
        pltpu.SMEM((requests,), jnp.int32),
        pltpu.SemaphoreType.DMA((items, GROUP)),
        pltpu.SemaphoreType.DMA((requests, width, capacity)),
        pltpu.SemaphoreType.DMA((items, 2)),
    ]
    if resume:
        scratch.append(pltpu.VMEM((items,) + blocks, jnp.bfloat16))
    if copy_pool:
        out_shape.append(jax.ShapeDtypeStruct(pool.shape, pool.dtype))
        parts = next(part for part in (6, 3, 2, 1) if pool.shape[1] % part == 0)
        scratch += [pltpu.VMEM(pool.shape, pool.dtype), pltpu.SemaphoreType.DMA((2, parts))]
    plan = dict(
        requests=requests, kv_heads=kv_heads, pages_listed=pages_listed, copy_pool=copy_pool,
        resume=resume,
    )
    return pl.pallas_call(
        lambda *refs: attend_kernel(plan, refs),
        out_shape=out_shape,
        in_specs=[SMEM, SMEM] + [ANY] * (requests + resume + 1),
        out_specs=[ANY] * len(out_shape),
        scratch_shapes=scratch,
        compiler_params=pltpu.CompilerParams(vmem_limit_bytes=VMEM_LIMIT),
        cost_estimate=cost(1.5 + 5.5 * items),
    )(me, tables, *asked, *([state] if resume else []), pool)


def project_kernel(shards, rank_ref, cos_ref, sin_ref, gain_ref, *refs):
    hidden_refs, weight_refs = refs[:shards], refs[shards : shards + 2]
    out_ref, features, gathered, feature_sem, weight_sem = refs[shards + 2 :]
    span = features.shape[2]
    width = weight_refs[0].shape[1]

    def copies(shard):
        rows = pl.ds(shard * span, span)
        return [
            pltpu.make_async_copy(
                weight_refs[kind].at[rows],
                gathered.at[rows, pl.ds(kind * width, width)],
                weight_sem.at[kind, shard],
            )
            for kind in range(2)
        ]

    for step in range(shards):
        shard = lax.rem(rank_ref[0] + shards - step, shards)
        pltpu.make_async_copy(hidden_refs[step], features.at[shard], feature_sem.at[step]).start()
    for shard in range(shards):
        for copy in copies(shard):
            copy.start()
    for step in range(shards):
        pltpu.make_async_copy(hidden_refs[step], features.at[0], feature_sem.at[step]).wait()
    raw = 0.0
    for shard in range(shards):
        for copy in copies(shard):
            copy.wait()
        raw = raw + plain_dot(features[shard], gathered[shard * span : (shard + 1) * span])
    columns = []
    for head in range(width // HD):
        one = raw[:, head * HD : (head + 1) * HD]
        mean = jnp.sum(one * one, axis=1, keepdims=True) * (1.0 / HD)
        one = one * lax.rsqrt(mean + 1e-06) * gain_ref[...]
        columns.append(one * cos_ref[...] + pltpu.roll(one, HD // 2, 1) * sin_ref[...])
    new_keys = jnp.concatenate(columns, axis=1) if len(columns) > 1 else columns[0]
    out_ref[0] = new_keys.astype(jnp.bfloat16)
    out_ref[1] = raw[:, width:].astype(jnp.bfloat16)


def project(rank, cos, sin, gain, hidden, weights):
    shards = len(hidden)
    new_count, span = hidden[0].shape
    depth, width = weights[0].shape
    vmem = pl.BlockSpec(memory_space=pltpu.VMEM)
    return pl.pallas_call(
        functools.partial(project_kernel, shards),
        out_shape=jax.ShapeDtypeStruct((2, new_count, width), jnp.bfloat16),
        in_specs=[SMEM, vmem, vmem, vmem] + [ANY] * (shards + 2),
        out_specs=vmem,
        scratch_shapes=[
            pltpu.VMEM((shards, new_count, span), jnp.bfloat16),
            pltpu.VMEM((depth, 2 * width), jnp.bfloat16),
            pltpu.SemaphoreType.DMA((shards,)),
            pltpu.SemaphoreType.DMA((2, shards)),
        ],
        compiler_params=pltpu.CompilerParams(vmem_limit_bytes=VMEM_LIMIT),
        cost_estimate=cost(5.0),
    )(rank, cos, sin, gain, *hidden, *weights)


def final_kernel(parts, q_ref, fresh_ref, *refs):
    states, partials, out_ref = refs[:2], refs[2 : 2 + parts], refs[-1]
    new_count = q_ref.shape[0]
    row = lax.broadcasted_iota(jnp.int32, (new_count, new_count), 0)
    column = lax.broadcasted_iota(jnp.int32, (new_count, new_count), 1)
    heads = [slice(head * HD, (head + 1) * HD) for head in range(GROUP)]
    stacked = jnp.concatenate([q_ref[:, span] for span in heads], axis=0)
    scores = row_dot(stacked, fresh_ref[0]).reshape(GROUP, new_count, new_count)
    scores = jnp.where((column <= row)[None], scores * SCALE, EMPTY)
    extras = [ref[0, GROUP].astype(jnp.bfloat16) for ref in states]
    weights, shares, divisors = [], [], []
    for head in range(GROUP):
        stats = [state_stats(extra, head) for extra in extras]
        stats += [(joined_stats(partial[0, GROUP], 3 * head), 1.0) for partial in partials]
        top = jnp.broadcast_to(jnp.max(scores[head], axis=1, keepdims=True), (new_count, HD))
        for other, _ in stats:
            top = jnp.maximum(top, other)
        pieces = [
            jnp.exp2(scores[head, :, start : start + HD] - top) for start in range(0, new_count, HD)
        ]
        total = jnp.broadcast_to(jnp.sum(sum(pieces), axis=1, keepdims=True), (new_count, HD))
        shares.append([jnp.exp2(other - top) for other, _ in stats])
        for share, (_, part) in zip(shares[-1], stats):
            total = total + share * part
        divisors.append(total)
        weights.append(jnp.concatenate(pieces, axis=1).astype(jnp.bfloat16))
    sums = plain_dot(jnp.concatenate(weights, axis=0), fresh_ref[1]).reshape(GROUP, new_count, HD)
    for head, span in enumerate(heads):
        mixed = sums[head]
        for share, ref in zip(shares[head], states + partials):
            mixed = mixed + share * ref[0, head].astype(jnp.float32)
        out_ref[:, span] = (mixed / divisors[head]).astype(jnp.bfloat16)


def final(kv_head, queries, fresh, states, partials, before):
    new_count = queries.shape[0]
    blocks = (1, GROUP + 1, new_count, HD)
    given = [] if before is None else [before]
    return pl.pallas_call(
        functools.partial(final_kernel, len(partials)),
        grid=(1,),
        out_shape=jax.ShapeDtypeStruct(queries.shape, jnp.bfloat16),
        in_specs=[
            pl.BlockSpec((new_count, BLOCK), lambda step: (0, kv_head)),
            pl.BlockSpec((2, new_count, HD), lambda step: (0, 0, kv_head)),
        ]
        + [pl.BlockSpec(blocks, lambda step: (0, 0, 0, 0))] * (len(states) + len(partials))
        + [ANY] * len(given),
        out_specs=pl.BlockSpec((new_count, BLOCK), lambda step: (0, kv_head)),
        input_output_aliases={2 + len(states) + len(partials): 0} if given else {},
        compiler_params=pltpu.CompilerParams(vmem_limit_bytes=VMEM_LIMIT),
        cost_estimate=cost(4.5),
    )(queries, fresh, *states, *partials, *given)


def write_kernel(holders, new_pages, base, me_ref, table_ref, *refs):
    pages = refs[:holders]
    out_ref, sem = refs[holders + 1], refs[holders + 2]
    me = me_ref[0]

    def each(action):
        for holder in range(holders):
            for page in range(new_pages):

                @pl.when(table_ref[holder, base + page] == me)
                def _(holder=holder, page=page):
                    slot = table_ref[holder, base + new_pages + page]
                    copy = pltpu.make_async_copy(
                        pages[holder].at[:, pl.ds(page * PAGE, PAGE)],
                        out_ref.at[:, slot],
                        sem.at[holder, page],
                    )
                    getattr(copy, action)()

    each("start")
    each("wait")


def write(me, tables, fresh, pool, new_pages, base):
    holders = len(fresh)
    return pl.pallas_call(
        functools.partial(write_kernel, holders, new_pages, base),
        out_shape=jax.ShapeDtypeStruct(pool.shape, pool.dtype),
        in_specs=[SMEM, SMEM]
        + [pl.BlockSpec(memory_space=pltpu.VMEM)] * holders
        + [ANY],
        out_specs=ANY,
        input_output_aliases={2 + holders: 0},
        scratch_shapes=[pltpu.SemaphoreType.DMA((holders, new_pages))],
        compiler_params=pltpu.CompilerParams(vmem_limit_bytes=VMEM_LIMIT),
        cost_estimate=cost(2.0),
    )(me, tables, *fresh, pool)


def per_device(
    hidden,
    k_weight,
    v_weight,
    k_gain,
    queries,
    kv_pool,
    page_holder,
    page_slot,
    page_count,
    write_owner,
    write_slot,
):
    inst_count = lax.axis_size("inst")
    shards = lax.axis_size("tp")
    me = lax.axis_index("inst").astype(jnp.int32)
    rank = lax.axis_index("tp").astype(jnp.int32)
    pages_listed = page_holder.shape[1]
    new_pages = write_owner.shape[1]
    capacity = 3 * pages_listed // (2 * inst_count)
    new_count = hidden.shape[0]
    kv_local = k_weight.shape[1] // HD
    me_list = me.reshape(1)

    def swap(array, step):
        return lax.ppermute(array, "inst", [(i, i ^ step) for i in range(inst_count)])

    def shift(array, step):
        return lax.ppermute(array, "tp", [(i, (i + step) % shards) for i in range(shards)])

    def after(array, *done):
        return lax.optimization_barrier((array,) + done)[0]

    heads = list(range(kv_local))
    base = 2 * pages_listed + 1
    own_table = jnp.concatenate(
        [page_holder[0], page_slot[0], page_count, write_owner[0], write_slot[0]]
    )
    own_table = jnp.pad(own_table, (0, 128 - own_table.shape[0]))[None]
    others = range(2, inst_count, 2)

    gathered = lax.all_gather(own_table, "inst", axis=0, tiled=True)
    sent = after(queries, gathered)
    asked = {0: queries, 1: swap(sent, 1)}
    for step in others:
        asked[step] = swap(sent, step)
    features = [hidden]
    for step in range(1, shards):
        features.append(shift(after(hidden, gathered), step))
    near, far = [features[1], features[-1]], features[2:-1]
    weights = [
        lax.all_gather(after(weight, gathered), "inst", axis=0, tiled=True)
        for weight in (k_weight, v_weight)
    ]
    tables = {
        step: lax.dynamic_slice_in_dim(gathered, me ^ step, 1, axis=0) for step in range(inst_count)
    }

    common = dict(pool=kv_pool, pages_listed=pages_listed, capacity=capacity)
    *found, pool_copy = attend(
        me_list, jnp.concatenate([tables[0], tables[1]]), [queries, asked[1]], heads,
        copy_pool=True, **common,
    )
    own_states, mate_states = found[:kv_local], found[kv_local:]
    last = mate_states[-1]

    partials = [[] for k in heads]
    for step in others:
        asked[step + 1] = swap(after(asked[step], last, *near), 1)
        begun = attend(
            me_list, after(tables[step + 1], last), [asked[step + 1]], heads, **common
        )
        last = begun[-1]
        halves = [swap(after(state, *far), 1) for state in begun]
        if step == 2:
            from_mate = [swap(after(state, last), 1) for state in mate_states]
        for k in heads:
            (last,) = attend(
                me_list, after(tables[step], last), [asked[step]], [k], state=halves[k],
                **common,
            )
            partials[k].append(swap(last, step))

    frequency = 1000000.0 ** (-(jnp.arange(HD // 2, dtype=jnp.float32) * 2.0) / HD)
    positions = page_count[0] * PAGE + jnp.arange(new_count, dtype=jnp.int32)
    angles = positions.astype(jnp.float32)[:, None] * frequency[None, :]
    cosine, sine = jnp.cos(angles), jnp.sin(angles)
    fresh = project(
        rank.reshape(1),
        jnp.concatenate([cosine, cosine], axis=1),
        jnp.concatenate([-sine, sine], axis=1),
        k_gain[None, :],
        [after(hidden, last)] + features[1:],
        weights,
    )
    attention_out = None
    for k in heads:
        attention_out = final(
            k, queries, fresh, [own_states[k], from_mate[k]], partials[k], attention_out
        )
    pages = {0: fresh, 1: swap(fresh, 1)}
    for step in range(2, inst_count, 2):
        pages[step] = swap(fresh, step)
        pages[step + 1] = swap(pages[step], 1)
    new_pool = write(
        me_list,
        jnp.concatenate([tables[step] for step in range(inst_count)]),
        [pages[step] for step in range(inst_count)],
        pool_copy,
        new_pages,
        base,
    )
    return (attention_out, new_pool)


def solution(mesh):
    return jax.shard_map(
        per_device,
        mesh=mesh,
        in_specs=(
            P(("groups", "inst"), "tp"),
            P("inst", "tp"),
            P("inst", "tp"),
            P(),
            P(("groups", "inst"), "tp"),
            P(None, ("groups", "inst"), None, "tp"),
            P(("groups", "inst"), None),
            P(("groups", "inst"), None),
            P(("groups", "inst")),
            P(("groups", "inst"), None),
            P(("groups", "inst"), None),
        ),
        out_specs=(P(("groups", "inst"), "tp"), P(None, ("groups", "inst"), None, "tp")),
        check_vma=False,
    )
```

profile of v0, /device:TPU:5, one launch (start us, length us, event | category | flops | bytes accessed | tf_op | source)
XLA Modules:
  0.0 149.7 jit_solution(2010514569025604318)
XLA Ops:
  7.9 0.8 concatenate.17
  8.6 5.5 %all-gather.1 = s32[4,1,128]{2,1,0:T(1,128)S(1)} all-gather(s32[1,1,128]{2,1,0:T(1,128)S(1)} %pad_bitcast_fusion), channel_id=2, replica_groups=mesh['groups'=2,'inst'=4,'tp'=4] {'inst'}, dimensions={0}, use_global_device_ids=true | all-gather | bytes 2560 | tf_op jit(solution)/shard_map/all_gather | solution.py:490
  14.4 1.3 collective-permute-start.1
  15.7 1.3 collective-permute-start.2
  17.0 2.0 %collective-permute-start.3 = (bf16[256,1280]{1,0:T(8,128)(2,1)}, bf16[256,1280]{1,0:T(8,128)(2,1)}, u32[]{:S(2)}, u32[]{:S(2)}) collective-permute-start(bf16[256,1280]{1,0:T(8,128)(2,1)} %refs_0_), channel_id=1, source_target_pairs={{0,3},{1,0},{2,1},{3,2},{4,7},{5,4},{6,5},{7,6},{8,11},{9,8},{10,9... | collective-permute-start | bytes 1966088 | tf_op jit(solution)/shard_map/ppermute | solution.py:477
  19.0 0.5 fusion.3
  19.6 0.6 pad_add_fusion.1.refs_1_
  20.1 29.1 %shard_map.122 = (f32[1,9,256,128]{3,2,1,0:T(8,128)}, f32[1,9,256,128]{3,2,1,0:T(8,128)}, f32[1,9,256,128]{3,2,1,0:T(8,128)}, f32[1,9,256,128]{3,2,1,0:T(8,128)}, bf16[2,54,128,256]{3,2,1,0:T(8,128)(2,1)}) custom-call(s32[1]{0:T(128)} %bitcast.3.refs_0_.me_ref, s32[2,128]{1,0:T(2,128)} %pad_add_fusion.1.refs_1_, bf16[256,2048]{1,0:T(8,128)(2,1)} %q_ref.3, ...), custom_call_target="tpu_custom_call" | custom-call | flops 23499999232 | bytes 70500000 | tf_op jit(solution)/shard_map/pallas_call | solution.py:282
  49.3 3.4 %collective-permute-done.1.refs_2_ = bf16[256,2048]{1,0:T(8,128)(2,1)} collective-permute-done((bf16[256,2048]{1,0:T(8,128)(2,1)}, bf16[256,2048]{1,0:T(8,128)(2,1)}, u32[]{:S(2)}, u32[]{:S(2)}) %collective-permute-start.1) | collective-permute-done | bytes 1048608 | tf_op jit(solution)/shard_map/ppermute | solution.py:474
  52.7 1.8 %collective-permute-start.4 = (bf16[256,2048]{1,0:T(8,128)(2,1)}, bf16[256,2048]{1,0:T(8,128)(2,1)}, u32[]{:S(2)}, u32[]{:S(2)}) collective-permute-start(bf16[256,2048]{1,0:T(8,128)(2,1)} %collective-permute-done.1.refs_2_), channel_id=1, source_target_pairs={{0,4},{4,0},{8,12},{12,8},{1,5},{5,1},{9,13},{13,9},{2,6},{6,2},{1... | collective-permute-start | bytes 3145736 | tf_op jit(solution)/shard_map/ppermute | solution.py:474
  54.5 2.4 %collective-permute-start.5 = (bf16[256,1280]{1,0:T(8,128)(2,1)S(1)}, bf16[256,1280]{1,0:T(8,128)(2,1)}, u32[]{:S(2)}, u32[]{:S(2)}) collective-permute-start(bf16[256,1280]{1,0:T(8,128)(2,1)S(1)} %copy-done.5), channel_id=1, source_target_pairs={{0,2},{1,3},{2,0},{3,1},{4,6},{5,7},{6,4},{7,5},{8,10},{9,11},{10,... | collective-permute-start | bytes 1966088 | tf_op jit(solution)/shard_map/ppermute | solution.py:477
  56.8 0.2 collective-permute-done.4.refs_2_
  57.1 13.5 %shard_map.123 = (f32[1,9,256,128]{3,2,1,0:T(8,128)}, f32[1,9,256,128]{3,2,1,0:T(8,128)}) custom-call(s32[1]{0:T(128)} %bitcast.3.refs_0_.me_ref, s32[1,128]{1,0:T(1,128)} %get-tuple-element.24.refs_1_, bf16[256,2048]{1,0:T(8,128)(2,1)} %collective-permute-done.4.refs_2_, bf16[2,54,128,256]{3,2,1,0:T(8,128)(2,1)} %refs_4_.5), custom_call_target="tpu_custom_call" | custom-call | flops 12499999744 | bytes 37500000 | tf_op jit(solution)/shard_map/pallas_call | solution.py:282
  70.6 15.4 %collective-permute-done.5.refs_2_ = bf16[256,1280]{1,0:T(8,128)(2,1)} collective-permute-done((bf16[256,1280]{1,0:T(8,128)(2,1)S(1)}, bf16[256,1280]{1,0:T(8,128)(2,1)}, u32[]{:S(2)}, u32[]{:S(2)}) %collective-permute-start.5) | collective-permute-done | bytes 655392 | tf_op jit(solution)/shard_map/ppermute | solution.py:477
  85.9 0.8 collective-permute-start.6
  86.8 0.6 pad_add_fusion.table_ref
  87.3 0.5 fusion
  87.9 0.8 pad_maximum_fusion
  88.7 0.5 collective-permute-start.8
  89.2 0.3 collective-permute-done.6.refs_3_
  89.5 8.3 %shard_map.124 = bf16[1,9,256,128]{3,2,1,0:T(8,128)(2,1)} custom-call(s32[1]{0:T(128)} %bitcast.3.refs_0_.me_ref, s32[1,128]{1,0:T(1,128)} %copy-done.3, bf16[256,2048]{1,0:T(8,128)(2,1)} %collective-permute-done.1.refs_2_, f32[1,9,256,128]{3,2,1,0:T(8,128)} %collective-permute-done.6.refs_3_, bf16[2,54,128,256]{3,2,1,0:T(8,128)(2,1)} %refs_4_.5), custom_call_target="tpu_custom_call" | custom-call | flops 7000000000 | bytes 21000000 | tf_op jit(solution)/shard_map/pallas_call | solution.py:282
  97.8 4.7 %collective-permute-start.11 = (bf16[1,9,256,128]{3,2,1,0:T(8,128)(2,1)}, bf16[1,9,256,128]{3,2,1,0:T(8,128)(2,1)}, u32[]{:S(2)}, u32[]{:S(2)}) collective-permute-start(bf16[1,9,256,128]{3,2,1,0:T(8,128)(2,1)} %shard_map.124), channel_id=1, source_target_pairs={{0,8},{4,12},{8,0},{12,4},{1,9},{5,13},{9,1},{13,5},{2,10},{6,14},... | collective-permute-start | bytes 1769480 | tf_op jit(solution)/shard_map/ppermute | solution.py:474
  102.6 8.4 %shard_map.125 = bf16[1,9,256,128]{3,2,1,0:T(8,128)(2,1)} custom-call(s32[1]{0:T(128)} %bitcast.3.refs_0_.me_ref, s32[1,128]{1,0:T(1,128)} %copy-done.3, bf16[256,2048]{1,0:T(8,128)(2,1)} %collective-permute-done.1.refs_2_, f32[1,9,256,128]{3,2,1,0:T(8,128)} %collective-permute-done.7.refs_3_, bf16[2,54,128,256]{3,2,1,0:T(8,128)(2,1)} %refs_4_.5), custom_call_target="tpu_custom_call" | custom-call | flops 7000000000 | bytes 21000000 | tf_op jit(solution)/shard_map/pallas_call | solution.py:282
  111.0 3.6 %collective-permute-start.9 = (bf16[1,9,256,128]{3,2,1,0:T(8,128)(2,1)}, bf16[1,9,256,128]{3,2,1,0:T(8,128)(2,1)}, u32[]{:S(2)}, u32[]{:S(2)}) collective-permute-start(bf16[1,9,256,128]{3,2,1,0:T(8,128)(2,1)} %shard_map.125), channel_id=1, source_target_pairs={{0,8},{4,12},{8,0},{12,4},{1,9},{5,13},{9,1},{13,5},{2,10},{6,14},... | collective-permute-start | bytes 1769480 | tf_op jit(solution)/shard_map/ppermute | solution.py:474
  114.5 6.9 %shard_map.126.fresh_ref.refs_0_ = bf16[2,256,256]{2,1,0:T(8,128)(2,1)} custom-call(s32[1]{0:T(128)} %bitcast.rank_ref, f32[256,128]{1,0:T(8,128)} %get-tuple-element.49.cos_ref, f32[256,128]{1,0:T(8,128)} %get-tuple-element.50.sin_ref, f32[1,128]{1,0:T(1,128)} %bitcast.23, bf16[256,1280]{1,0:T(8,128)(2,1)} %refs_0_, ...), custom_call_target="tpu_custom_call" | custom-call | flops 5000000000 | bytes 15000000 | tf_op jit(solution)/shard_map/pallas_call | solution.py:339
  121.5 0.9 collective-permute-start.13
  122.4 4.7 %shard_map.127.refs_3_ = bf16[256,2048]{1,0:T(8,128)(2,1)} custom-call(bf16[256,2048]{1,0:T(8,128)(2,1)} %q_ref.3, bf16[2,256,256]{2,1,0:T(8,128)(2,1)} %shard_map.126.fresh_ref.refs_0_, f32[1,9,256,128]{3,2,1,0:T(8,128)} %get-tuple-element.38.refs_0_, f32[1,9,256,128]{3,2,1,0:T(8,128)} %collective-permute-done.10.refs_1_, ...), custom_call_target="tpu_custom_call" | custom-call | flops 4499999744 | bytes 13500000 | tf_op jit(solution)/shard_map/pallas_call | solution.py:393
  127.2 7.1 %collective-permute-done.13.refs_2_ = bf16[2,256,256]{2,1,0:T(8,128)(2,1)S(1)} collective-permute-done((bf16[2,256,256]{2,1,0:T(8,128)(2,1)}, bf16[2,256,256]{2,1,0:T(8,128)(2,1)S(1)}, u32[]{:S(2)}, u32[]{:S(2)}) %collective-permute-start.13) | collective-permute-done | bytes 262176 | tf_op jit(solution)/shard_map/ppermute | solution.py:474
  134.3 1.0 collective-permute-start.14
  135.3 4.7 %shard_map.128 = bf16[256,2048]{1,0:T(8,128)(2,1)} custom-call(bf16[256,2048]{1,0:T(8,128)(2,1)} %q_ref.3, bf16[2,256,256]{2,1,0:T(8,128)(2,1)} %shard_map.126.fresh_ref.refs_0_, f32[1,9,256,128]{3,2,1,0:T(8,128)} %get-tuple-element.36.refs_0_, f32[1,9,256,128]{3,2,1,0:T(8,128)} %collective-permute-done.8.refs_1_, ...), custom_call_target="tpu_custom_call", output_to_operand_aliasing={{}: (5, {})} | custom-call | flops 4499999744 | bytes 13500000 | tf_op jit(solution)/shard_map/pallas_call | solution.py:393
  140.1 0.7 copy-done
  140.9 2.0 %shard_map.129 = bf16[2,54,128,256]{3,2,1,0:T(8,128)(2,1)} custom-call(s32[1]{0:T(128)} %bitcast.3.refs_0_.me_ref, s32[4,128]{1,0:T(4,128)} %pad_add_fusion.table_ref, bf16[2,256,256]{2,1,0:T(8,128)(2,1)} %shard_map.126.fresh_ref.refs_0_, bf16[2,256,256]{2,1,0:T(8,128)(2,1)} %copy-done, ...), custom_call_target="tpu_custom_call", output_to_operand_aliasing={{}: (6, {})} | custom-call | flops 2000000000 | bytes 6000000 | tf_op jit(solution)/shard_map/pallas_call | solution.py:435
  (34 shorter events, 0.6 us)
Async XLA Ops:
  7.2 107.3 %all-gather.5.cloned.1.call-start = ((), (), s32[]{:S(2)}) async-start(), calls=%async_computation | async-start | bytes 3276800 | tf_op jit(solution)/shard_map/all_gather | solution.py:500
  14.1 6.0 %collective-permute-start = (bf16[256,2048]{1,0:T(8,128)(2,1)}, bf16[256,2048]{1,0:T(8,128)(2,1)}, u32[]{:S(2)}, u32[]{:S(2)}) collective-permute-start(bf16[256,2048]{1,0:T(8,128)(2,1)} %q_ref.3), channel_id=1, source_target_pairs={{0,4},{4,0},{8,12},{12,8},{1,5},{5,1},{9,13},{13,9},{2,6},{6,2},{1... | collective-permute-start | bytes 3145736 | tf_op jit(solution)/shard_map/ppermute | solution.py:474
  14.4 100.1 %all-gather.7.cloned.1.call-start = ((), (), s32[]{:S(2)}) async-start(), calls=%async_computation.1 | async-start | bytes 3276800 | tf_op jit(solution)/shard_map/all_gather | solution.py:500
  14.4 38.2 %collective-permute-start.1 = (bf16[256,2048]{1,0:T(8,128)(2,1)}, bf16[256,2048]{1,0:T(8,128)(2,1)}, u32[]{:S(2)}, u32[]{:S(2)}) collective-permute-start(bf16[256,2048]{1,0:T(8,128)(2,1)} %q_ref.3), channel_id=1, source_target_pairs={{0,8},{4,12},{8,0},{12,4},{1,9},{5,13},{9,1},{13,5},{2,10},{6,14},... | collective-permute-start | bytes 3145736 | tf_op jit(solution)/shard_map/ppermute | solution.py:474
  15.7 33.6 %collective-permute-start.2 = (bf16[256,1280]{1,0:T(8,128)(2,1)}, bf16[256,1280]{1,0:T(8,128)(2,1)}, u32[]{:S(2)}, u32[]{:S(2)}) collective-permute-start(bf16[256,1280]{1,0:T(8,128)(2,1)} %refs_0_), channel_id=1, source_target_pairs={{0,1},{1,2},{2,3},{3,0},{4,5},{5,6},{6,7},{7,4},{8,9},{9,10},{10,1... | collective-permute-start | bytes 1966088 | tf_op jit(solution)/shard_map/ppermute | solution.py:477
  17.0 32.3 %collective-permute-start.3 = (bf16[256,1280]{1,0:T(8,128)(2,1)}, bf16[256,1280]{1,0:T(8,128)(2,1)}, u32[]{:S(2)}, u32[]{:S(2)}) collective-permute-start(bf16[256,1280]{1,0:T(8,128)(2,1)} %refs_0_), channel_id=1, source_target_pairs={{0,3},{1,0},{2,1},{3,2},{4,7},{5,4},{6,5},{7,6},{8,11},{9,8},{10,9... | collective-permute-start | bytes 1966088 | tf_op jit(solution)/shard_map/ppermute | solution.py:477
  19.5 67.2 %copy-start.3 = (s32[1,128]{1,0:T(1,128)}, s32[1,128]{1,0:T(1,128)S(1)}, u32[]{:S(2)}) copy-start(s32[1,128]{1,0:T(1,128)S(1)} %get-tuple-element.31.refs_1_) | copy-start | bytes 1540
  20.1 34.3 %copy-start.5 = (bf16[256,1280]{1,0:T(8,128)(2,1)S(1)}, bf16[256,1280]{1,0:T(8,128)(2,1)}, u32[]{:S(2)}) copy-start(bf16[256,1280]{1,0:T(8,128)(2,1)} %refs_0_) | copy-start | bytes 1966084
  52.7 4.4 %collective-permute-start.4 = (bf16[256,2048]{1,0:T(8,128)(2,1)}, bf16[256,2048]{1,0:T(8,128)(2,1)}, u32[]{:S(2)}, u32[]{:S(2)}) collective-permute-start(bf16[256,2048]{1,0:T(8,128)(2,1)} %collective-permute-done.1.refs_2_), channel_id=1, source_target_pairs={{0,4},{4,0},{8,12},{12,8},{1,5},{5,1},{9,13},{13,9},{2,6},{6,2},{1... | collective-permute-start | bytes 3145736 | tf_op jit(solution)/shard_map/ppermute | solution.py:474
  54.5 31.5 %collective-permute-start.5 = (bf16[256,1280]{1,0:T(8,128)(2,1)S(1)}, bf16[256,1280]{1,0:T(8,128)(2,1)}, u32[]{:S(2)}, u32[]{:S(2)}) collective-permute-start(bf16[256,1280]{1,0:T(8,128)(2,1)S(1)} %copy-done.5), channel_id=1, source_target_pairs={{0,2},{1,3},{2,0},{3,1},{4,6},{5,7},{6,4},{7,5},{8,10},{9,11},{10,... | collective-permute-start | bytes 1966088 | tf_op jit(solution)/shard_map/ppermute | solution.py:477
  56.8 29.9 %copy-start.4 = (s32[1,128]{1,0:T(1,128)S(1)}, s32[1,128]{1,0:T(1,128)}, u32[]{:S(2)}) copy-start(s32[1,128]{1,0:T(1,128)} %get-tuple-element.24.refs_1_) | copy-start | bytes 1540
  85.9 3.6 %collective-permute-start.6 = (f32[1,9,256,128]{3,2,1,0:T(8,128)}, f32[1,9,256,128]{3,2,1,0:T(8,128)}, u32[]{:S(2)}, u32[]{:S(2)}) collective-permute-start(f32[1,9,256,128]{3,2,1,0:T(8,128)} %get-tuple-element.30), channel_id=1, source_target_pairs={{0,4},{4,0},{8,12},{12,8},{1,5},{5,1},{9,13},{13,9},{2,6},{6,2},{1... | collective-permute-start | bytes 3538952 | tf_op jit(solution)/shard_map/ppermute | solution.py:474
  86.7 15.9 %collective-permute-start.7 = (f32[1,9,256,128]{3,2,1,0:T(8,128)}, f32[1,9,256,128]{3,2,1,0:T(8,128)}, u32[]{:S(2)}, u32[]{:S(2)}) collective-permute-start(f32[1,9,256,128]{3,2,1,0:T(8,128)} %get-tuple-element.32), channel_id=1, source_target_pairs={{0,4},{4,0},{8,12},{12,8},{1,5},{5,1},{9,13},{13,9},{2,6},{6,2},{1... | collective-permute-start | bytes 3538952 | tf_op jit(solution)/shard_map/ppermute | solution.py:474
  88.7 46.6 %collective-permute-start.8 = (f32[1,9,256,128]{3,2,1,0:T(8,128)}, f32[1,9,256,128]{3,2,1,0:T(8,128)}, u32[]{:S(2)}, u32[]{:S(2)}) collective-permute-start(f32[1,9,256,128]{3,2,1,0:T(8,128)} %get-tuple-element.37), channel_id=1, source_target_pairs={{0,4},{4,0},{8,12},{12,8},{1,5},{5,1},{9,13},{13,9},{2,6},{6,2},{1... | collective-permute-start | bytes 3538952 | tf_op jit(solution)/shard_map/ppermute | solution.py:474
  89.2 32.3 %collective-permute-start.10 = (f32[1,9,256,128]{3,2,1,0:T(8,128)}, f32[1,9,256,128]{3,2,1,0:T(8,128)}, u32[]{:S(2)}, u32[]{:S(2)}) collective-permute-start(f32[1,9,256,128]{3,2,1,0:T(8,128)} %get-tuple-element.40), channel_id=1, source_target_pairs={{0,4},{4,0},{8,12},{12,8},{1,5},{5,1},{9,13},{13,9},{2,6},{6,2},{1... | collective-permute-start | bytes 3538952 | tf_op jit(solution)/shard_map/ppermute | solution.py:474
  97.8 24.6 %collective-permute-start.11 = (bf16[1,9,256,128]{3,2,1,0:T(8,128)(2,1)}, bf16[1,9,256,128]{3,2,1,0:T(8,128)(2,1)}, u32[]{:S(2)}, u32[]{:S(2)}) collective-permute-start(bf16[1,9,256,128]{3,2,1,0:T(8,128)(2,1)} %shard_map.124), channel_id=1, source_target_pairs={{0,8},{4,12},{8,0},{12,4},{1,9},{5,13},{9,1},{13,5},{2,10},{6,14},... | collective-permute-start | bytes 1769480 | tf_op jit(solution)/shard_map/ppermute | solution.py:474
  111.0 24.4 %collective-permute-start.9 = (bf16[1,9,256,128]{3,2,1,0:T(8,128)(2,1)}, bf16[1,9,256,128]{3,2,1,0:T(8,128)(2,1)}, u32[]{:S(2)}, u32[]{:S(2)}) collective-permute-start(bf16[1,9,256,128]{3,2,1,0:T(8,128)(2,1)} %shard_map.125), channel_id=1, source_target_pairs={{0,8},{4,12},{8,0},{12,4},{1,9},{5,13},{9,1},{13,5},{2,10},{6,14},... | collective-permute-start | bytes 1769480 | tf_op jit(solution)/shard_map/ppermute | solution.py:474
  121.4 18.6 %collective-permute-start.12 = (bf16[2,256,256]{2,1,0:T(8,128)(2,1)}, bf16[2,256,256]{2,1,0:T(8,128)(2,1)S(1)}, u32[]{:S(2)}, u32[]{:S(2)}) collective-permute-start(bf16[2,256,256]{2,1,0:T(8,128)(2,1)} %shard_map.126.fresh_ref.refs_0_), channel_id=1, source_target_pairs={{0,4},{4,0},{8,12},{12,8},{1,5},{5,1},{9,13},{13,9},{2,6},{6,2},{1... | collective-permute-start | bytes 786440 | tf_op jit(solution)/shard_map/ppermute | solution.py:474
  121.5 12.8 %collective-permute-start.13 = (bf16[2,256,256]{2,1,0:T(8,128)(2,1)}, bf16[2,256,256]{2,1,0:T(8,128)(2,1)S(1)}, u32[]{:S(2)}, u32[]{:S(2)}) collective-permute-start(bf16[2,256,256]{2,1,0:T(8,128)(2,1)} %shard_map.126.fresh_ref.refs_0_), channel_id=1, source_target_pairs={{0,8},{4,12},{8,0},{12,4},{1,9},{5,13},{9,1},{13,5},{2,10},{6,14},... | collective-permute-start | bytes 786440 | tf_op jit(solution)/shard_map/ppermute | solution.py:474
  134.3 5.8 %copy-start.1 = (bf16[2,256,256]{2,1,0:T(8,128)(2,1)}, bf16[2,256,256]{2,1,0:T(8,128)(2,1)S(1)}, u32[]{:S(2)}) copy-start(bf16[2,256,256]{2,1,0:T(8,128)(2,1)S(1)} %collective-permute-done.13.refs_2_) | copy-start | bytes 786436
  134.3 5.8 %collective-permute-start.14 = (bf16[2,256,256]{2,1,0:T(8,128)(2,1)S(1)}, bf16[2,256,256]{2,1,0:T(8,128)(2,1)S(1)}, u32[]{:S(2)}, u32[]{:S(2)}) collective-permute-start(bf16[2,256,256]{2,1,0:T(8,128)(2,1)S(1)} %collective-permute-done.13.refs_2_), channel_id=1, source_target_pairs={{0,4},{4,0},{8,12},{12,8},{1,5},{5,1},{9,13},{13,9},{2,6},{6,2},{1... | collective-permute-start | bytes 786440 | tf_op jit(solution)/shard_map/ppermute | solution.py:474
  140.1 0.7 copy-start
  140.1 0.8 copy-start.2
Sparse Core Ops, SparseCore 0:
  14.5 40.6 all-gather.4
  56.7 25.8 all-gather.6
where the time goes:
time: 149 us; the launch traced here: 150 us
  Pallas kernels  77.7 us (52%)
  waiting for transfers between devices  26.4 us (18%)
  starting transfers between devices  20.6 us (14%)
  between operations  14.8 us (10%)
  blocking collectives  5.49 us (4%)
  other arithmetic  2.53 us (2%)
  local copies, waits for them, and re-layouts  2.08 us (1%)
    pallas_call x4, Pallas kernels, attend(): pl.pallas_call(lambda *refs: attend_kernel(plan, refs), out_shape=out_sha...  59.3 us
    ppermute x3, waiting for transfers between devices, shift(): lax.ppermute(array, 'tp', [(i, (i + step) % shards) for i in range(shards)])  15.4 us
    ppermute x12, starting transfers between devices, swap(): lax.ppermute(array, 'inst', [(i, i ^ step) for i in range(inst_count)])  14.9 us
    ppermute x12, waiting for transfers between devices, swap(): lax.ppermute(array, 'inst', [(i, i ^ step) for i in range(inst_count)])  11 us
    pallas_call x2, Pallas kernels, final(): pl.pallas_call(functools.partial(final_kernel, len(partials)), grid=(1,),...  9.45 us
    pallas_call x1, Pallas kernels, project(): pl.pallas_call(functools.partial(project_kernel, shards), out_shape=jax.S...  6.92 us
    ppermute x3, starting transfers between devices, shift(): lax.ppermute(array, 'tp', [(i, (i + step) % shards) for i in range(shards)])  5.7 us
    all_gather x1, blocking collectives, per_device(): gathered = lax.all_gather(own_table, 'inst', axis=0, tiled=True)  5.49 us
  transfers between devices with their start and end apart: 17, of which 5 were waited for; matrix products, arithmetic and copies ran while one was open for 2% of the time, Pallas kernels for 51%

commit v1 on v0

--- a/solution.py
+++ b/solution.py
@@ -57,7 +57,8 @@
 
 
 def attend_kernel(plan, refs):
-    requests, kv_heads, pages_listed = plan["requests"], plan["kv_heads"], plan["pages_listed"]
+    steps, kv_heads, pages_listed = plan["steps"], plan["kv_heads"], plan["pages_listed"]
+    requests = len(steps)
     copy_pool, resume = plan["copy_pool"], plan["resume"]
     width = len(kv_heads)
     items = requests * width
@@ -112,15 +113,16 @@
         state_copy = pltpu.make_async_copy(state_ref, acc, out_sem.at[0, 0])
         state_copy.start()
     me = me_ref[0]
-    for request in range(requests):
-        count = table_ref[request, 2 * pages_listed]
-
-        def look(page, found, request=request, count=count):
-            mine = (page < count) & (table_ref[request, page] == me)
+    for request, apart in enumerate(steps):
+        whose = me ^ apart
+        count = table_ref[whose, 2 * pages_listed]
+
+        def look(page, found, request=request, whose=whose, count=count):
+            mine = (page < count) & (table_ref[whose, page] == me)
 
             @pl.when(mine)
             def _():
-                for copy in page_copies(request, found, table_ref[request, pages_listed + page]):
+                for copy in page_copies(request, found, table_ref[whose, pages_listed + page]):
                     copy.start()
 
             return found + mine.astype(jnp.int32)
@@ -251,8 +253,10 @@
         copy.wait()
 
 
-def attend(me, tables, asked, kv_heads, pool, pages_listed, capacity, state=None, copy_pool=False):
-    requests, width, new_count = tables.shape[0], len(kv_heads), asked[0].shape[0]
+def attend(
+    me, tables, steps, asked, kv_heads, pool, pages_listed, capacity, takes, state=None, copy_pool=False
+):
+    requests, width, new_count = len(steps), len(kv_heads), asked[0].shape[0]
     items = requests * width
     resume = state is not None
     blocks = (GROUP + 1, new_count, HD)
@@ -276,7 +280,7 @@
         parts = next(part for part in (6, 3, 2, 1) if pool.shape[1] % part == 0)
         scratch += [pltpu.VMEM(pool.shape, pool.dtype), pltpu.SemaphoreType.DMA((2, parts))]
     plan = dict(
-        requests=requests, kv_heads=kv_heads, pages_listed=pages_listed, copy_pool=copy_pool,
+        steps=steps, kv_heads=kv_heads, pages_listed=pages_listed, copy_pool=copy_pool,
         resume=resume,
     )
     return pl.pallas_call(
@@ -286,39 +290,39 @@
         out_specs=[ANY] * len(out_shape),
         scratch_shapes=scratch,
         compiler_params=pltpu.CompilerParams(vmem_limit_bytes=VMEM_LIMIT),
-        cost_estimate=cost(1.5 + 5.5 * items),
+        cost_estimate=cost(takes),
     )(me, tables, *asked, *([state] if resume else []), pool)
 
 
-def project_kernel(shards, rank_ref, cos_ref, sin_ref, gain_ref, *refs):
-    hidden_refs, weight_refs = refs[:shards], refs[shards : shards + 2]
-    out_ref, features, gathered, feature_sem, weight_sem = refs[shards + 2 :]
+def project_kernel(shards, holders, rank_ref, cos_ref, sin_ref, gain_ref, *refs):
+    hidden_refs, weight_ref = refs[:shards], refs[shards]
+    out_ref, features, gathered, feature_sem, weight_sem = refs[shards + 1 :]
     span = features.shape[2]
-    width = weight_refs[0].shape[1]
-
-    def copies(shard):
-        rows = pl.ds(shard * span, span)
-        return [
-            pltpu.make_async_copy(
-                weight_refs[kind].at[rows],
-                gathered.at[rows, pl.ds(kind * width, width)],
-                weight_sem.at[kind, shard],
-            )
-            for kind in range(2)
-        ]
+    depth, width = gathered.shape[0], gathered.shape[1] // 2
+    groups = weight_sem.shape[0]
+    rows = depth // (groups * holders)
+
+    def copy(group, holder):
+        return pltpu.make_async_copy(
+            weight_ref.at[pl.ds((group * holders + holder) * rows, rows)],
+            gathered.at[pl.ds((holder * groups + group) * rows, rows)],
+            weight_sem.at[group, holder],
+        )
 
     for step in range(shards):
         shard = lax.rem(rank_ref[0] + shards - step, shards)
         pltpu.make_async_copy(hidden_refs[step], features.at[shard], feature_sem.at[step]).start()
-    for shard in range(shards):
-        for copy in copies(shard):
-            copy.start()
+    for holder in range(holders):
+        for group in range(groups):
+            copy(group, holder).start()
     for step in range(shards):
         pltpu.make_async_copy(hidden_refs[step], features.at[0], feature_sem.at[step]).wait()
     raw = 0.0
     for shard in range(shards):
-        for copy in copies(shard):
-            copy.wait()
+        for holder in range(holders):
+            if holder * groups * rows // span == shard:
+                for group in range(groups):
+                    copy(group, holder).wait()
         raw = raw + plain_dot(features[shard], gathered[shard * span : (shard + 1) * span])
     columns = []
     for head in range(width // HD):
@@ -331,25 +335,24 @@
     out_ref[1] = raw[:, width:].astype(jnp.bfloat16)
 
 
-def project(rank, cos, sin, gain, hidden, weights):
+def project(rank, cos, sin, gain, hidden, weight, groups, holders):
     shards = len(hidden)
     new_count, span = hidden[0].shape
-    depth, width = weights[0].shape
     vmem = pl.BlockSpec(memory_space=pltpu.VMEM)
     return pl.pallas_call(
-        functools.partial(project_kernel, shards),
-        out_shape=jax.ShapeDtypeStruct((2, new_count, width), jnp.bfloat16),
-        in_specs=[SMEM, vmem, vmem, vmem] + [ANY] * (shards + 2),
+        functools.partial(project_kernel, shards, holders),
+        out_shape=jax.ShapeDtypeStruct((2, new_count, weight.shape[1] // 2), jnp.bfloat16),
+        in_specs=[SMEM, vmem, vmem, vmem] + [ANY] * (shards + 1),
         out_specs=vmem,
         scratch_shapes=[
             pltpu.VMEM((shards, new_count, span), jnp.bfloat16),
-            pltpu.VMEM((depth, 2 * width), jnp.bfloat16),
+            pltpu.VMEM(weight.shape, weight.dtype),
             pltpu.SemaphoreType.DMA((shards,)),
-            pltpu.SemaphoreType.DMA((2, shards)),
+            pltpu.SemaphoreType.DMA((groups, holders)),
         ],
         compiler_params=pltpu.CompilerParams(vmem_limit_bytes=VMEM_LIMIT),
-        cost_estimate=cost(5.0),
-    )(rank, cos, sin, gain, *hidden, *weights)
+        cost_estimate=cost(0.2),
+    )(rank, cos, sin, gain, *hidden, weight)
 
 
 def final_kernel(parts, q_ref, fresh_ref, *refs):
@@ -403,7 +406,7 @@
         out_specs=pl.BlockSpec((new_count, BLOCK), lambda step: (0, kv_head)),
         input_output_aliases={2 + len(states) + len(partials): 0} if given else {},
         compiler_params=pltpu.CompilerParams(vmem_limit_bytes=VMEM_LIMIT),
-        cost_estimate=cost(4.5),
+        cost_estimate=cost(0.2),
     )(queries, fresh, *states, *partials, *given)
 
 
@@ -416,9 +419,9 @@
         for holder in range(holders):
             for page in range(new_pages):
 
-                @pl.when(table_ref[holder, base + page] == me)
+                @pl.when(table_ref[me ^ holder, base + page] == me)
                 def _(holder=holder, page=page):
-                    slot = table_ref[holder, base + new_pages + page]
+                    slot = table_ref[me ^ holder, base + new_pages + page]
                     copy = pltpu.make_async_copy(
                         pages[holder].at[:, pl.ds(page * PAGE, PAGE)],
                         out_ref.at[:, slot],
@@ -442,7 +445,7 @@
         input_output_aliases={2 + holders: 0},
         scratch_shapes=[pltpu.SemaphoreType.DMA((holders, new_pages))],
         compiler_params=pltpu.CompilerParams(vmem_limit_bytes=VMEM_LIMIT),
-        cost_estimate=cost(2.0),
+        cost_estimate=cost(0.2),
     )(me, tables, *fresh, pool)
 
 
@@ -463,6 +466,8 @@
     shards = lax.axis_size("tp")
     me = lax.axis_index("inst").astype(jnp.int32)
     rank = lax.axis_index("tp").astype(jnp.int32)
+    groups = lax.axis_size("groups")
+    group = lax.axis_index("groups").astype(jnp.int32)
     pages_listed = page_holder.shape[1]
     new_pages = write_owner.shape[1]
     capacity = 3 * pages_listed // (2 * inst_count)
@@ -487,72 +492,83 @@
     own_table = jnp.pad(own_table, (0, 128 - own_table.shape[0]))[None]
     others = range(2, inst_count, 2)
 
-    gathered = lax.all_gather(own_table, "inst", axis=0, tiled=True)
-    sent = after(queries, gathered)
+    tables = lax.all_gather(own_table, "inst", axis=0, tiled=True)
+    sent = after(queries, tables)
     asked = {0: queries, 1: swap(sent, 1)}
     for step in others:
         asked[step] = swap(sent, step)
     features = [hidden]
+    forwarded = shards == 4
     for step in range(1, shards):
-        features.append(shift(after(hidden, gathered), step))
-    near, far = [features[1], features[-1]], features[2:-1]
-    weights = [
-        lax.all_gather(after(weight, gathered), "inst", axis=0, tiled=True)
-        for weight in (k_weight, v_weight)
-    ]
-    tables = {
-        step: lax.dynamic_slice_in_dim(gathered, me ^ step, 1, axis=0) for step in range(inst_count)
-    }
+        direct = not forwarded or step != 2
+        features.append(shift(after(hidden, tables), step) if direct else None)
+    near = [features[1], features[-1]]
+    share = k_weight.shape[0] // groups
+    weight = jnp.concatenate(
+        [lax.dynamic_slice_in_dim(one, group * share, share) for one in (k_weight, v_weight)],
+        axis=1,
+    )
+    weight = lax.all_gather(after(weight, tables), ("groups", "inst"), axis=0, tiled=True)
 
     common = dict(pool=kv_pool, pages_listed=pages_listed, capacity=capacity)
     *found, pool_copy = attend(
-        me_list, jnp.concatenate([tables[0], tables[1]]), [queries, asked[1]], heads,
-        copy_pool=True, **common,
+        me_list, tables, [0, 1], [queries, asked[1]], heads, copy_pool=True, takes=22.0, **common
     )
     own_states, mate_states = found[:kv_local], found[kv_local:]
     last = mate_states[-1]
-
-    partials = [[] for k in heads]
-    for step in others:
-        asked[step + 1] = swap(after(asked[step], last, *near), 1)
-        begun = attend(
-            me_list, after(tables[step + 1], last), [asked[step + 1]], heads, **common
-        )
-        last = begun[-1]
-        halves = [swap(after(state, *far), 1) for state in begun]
-        if step == 2:
-            from_mate = [swap(after(state, last), 1) for state in mate_states]
-        for k in heads:
-            (last,) = attend(
-                me_list, after(tables[step], last), [asked[step]], [k], state=halves[k],
-                **common,
-            )
-            partials[k].append(swap(last, step))
 
     frequency = 1000000.0 ** (-(jnp.arange(HD // 2, dtype=jnp.float32) * 2.0) / HD)
     positions = page_count[0] * PAGE + jnp.arange(new_count, dtype=jnp.int32)
     angles = positions.astype(jnp.float32)[:, None] * frequency[None, :]
     cosine, sine = jnp.cos(angles), jnp.sin(angles)
-    fresh = project(
-        rank.reshape(1),
-        jnp.concatenate([cosine, cosine], axis=1),
-        jnp.concatenate([-sine, sine], axis=1),
-        k_gain[None, :],
-        [after(hidden, last)] + features[1:],
-        weights,
-    )
+    partials = [[] for k in heads]
+    fresh = None
+    for step in others:
+        asked[step + 1] = swap(after(asked[step], last, *near), 1)
+        if forwarded and features[2] is None:
+            ahead = lax.ppermute(after(features[1], last), "tp", [(1, 2), (2, 3)])
+            back = lax.ppermute(after(features[3], last), "tp", [(1, 0), (2, 1)])
+            features[2] = jnp.where(rank >= 2, ahead, back)
+            near = [ahead, back]
+        begun = attend(
+            me_list, after(tables, last), [step + 1], [asked[step + 1]], heads, takes=12.0, **common
+        )
+        last = begun[-1]
+        halves = [swap(after(state, *near), 1) for state in begun]
+        if fresh is None:
+            from_mate = [swap(after(state, last), 1) for state in mate_states]
+            fresh = project(
+                rank.reshape(1),
+                jnp.concatenate([cosine, cosine], axis=1),
+                jnp.concatenate([-sine, sine], axis=1),
+                k_gain[None, :],
+                [after(hidden, last)] + features[1:],
+                weight,
+                groups,
+                inst_count,
+            )
+            last = fresh
+            pages = {0: fresh, 1: swap(fresh, 1)}
+            for apart in others:
+                pages[apart] = swap(fresh, apart)
+        for k in heads:
+            sent_first = [pages[apart] for apart in others] if k > 0 else []
+            (last,) = attend(
+                me_list, after(tables, last, *sent_first), [step], [asked[step]], [k],
+                state=halves[k], takes=0.2, **common,
+            )
+            partials[k].append(swap(last, step))
+
     attention_out = None
     for k in heads:
         attention_out = final(
-            k, queries, fresh, [own_states[k], from_mate[k]], partials[k], attention_out
+            k, after(queries, last), fresh, [own_states[k], from_mate[k]], partials[k], attention_out
         )
-    pages = {0: fresh, 1: swap(fresh, 1)}
-    for step in range(2, inst_count, 2):
-        pages[step] = swap(fresh, step)
-        pages[step + 1] = swap(pages[step], 1)
+    for step in others:
+        pages[step + 1] = swap(after(pages[step], last), 1)
     new_pool = write(
         me_list,
-        jnp.concatenate([tables[step] for step in range(inst_count)]),
+        tables,
         [pages[step] for step in range(inst_count)],
         pool_copy,
         new_pages,

time: 149 us -> 139 us (0.933); the launches traced: 150 us -> 137 us
  waiting for transfers between devices: 26.4 us -> 9.58 us
  local copies, waits for them, and re-layouts: 2.08 us -> 4.83 us
  other arithmetic: 2.53 us -> 4.28 us
    ppermute x3 -> x2, waiting for transfers between devices: 15.4 us -> 5.03 us  [shift(): lax.ppermute(array, 'tp', [(i, (i + step) % shards) for i in range(shards)])]
    ppermute x12, waiting for transfers between devices: 11 us -> 4.52 us  [swap(): lax.ppermute(array, 'inst', [(i, i ^ step) for i in range(inst_count)])]
    ppermute x3 -> x2, starting transfers between devices: 5.7 us -> 3.32 us  [shift(): lax.ppermute(array, 'tp', [(i, (i + step) % shards) for i in range(shards)])]
    unnamed x13, local copies, waits for them, and re-layouts: 0.78 us -> 2.94 us
    select_n x0 -> x1, other arithmetic: none -> 1.99 us  [per_device(): features[2] = jnp.where(rank >= 2, ahead, back)]
    ppermute x0 -> x2, starting transfers between devices: none -> 1.98 us  [the longest x1 1.29 us: per_device(): back = lax.ppermute(after(features[3], last), 'tp', [(1, 0), (2, 1)])]
  transfers between devices with their start and end apart: 17 -> 17, of which waited for: 5 -> 5; matrix products, arithmetic and copies ran while one was open for 2% -> 2% of each run, Pallas kernels for 51% -> 54%
where the time goes in v1:
time: 139 us; the launch traced here: 137 us
  Pallas kernels  78.4 us (56%)
  starting transfers between devices  19.4 us (14%)
  between operations  14.8 us (11%)
  waiting for transfers between devices  9.58 us (7%)
  blocking collectives  5.49 us (4%)
  local copies, waits for them, and re-layouts  4.83 us (3%)
  other arithmetic  4.28 us (3%)
    pallas_call x4, Pallas kernels, attend(): pl.pallas_call(lambda *refs: attend_kernel(plan, refs), out_shape=out_sha...  60.1 us
    ppermute x12, starting transfers between devices, swap(): lax.ppermute(array, 'inst', [(i, i ^ step) for i in range(inst_count)])  14.1 us
    pallas_call x2, Pallas kernels, final(): pl.pallas_call(functools.partial(final_kernel, len(partials)), grid=(1,),...  9.46 us
    pallas_call x1, Pallas kernels, project(): pl.pallas_call(functools.partial(project_kernel, shards, holders), out_sh...  6.93 us
    all_gather x1, blocking collectives, per_device(): tables = lax.all_gather(own_table, 'inst', axis=0, tiled=True)  5.49 us
    ppermute x2, waiting for transfers between devices, shift(): lax.ppermute(array, 'tp', [(i, (i + step) % shards) for i in range(shards)])  5.03 us
    ppermute x12, waiting for transfers between devices, swap(): lax.ppermute(array, 'inst', [(i, i ^ step) for i in range(inst_count)])  4.52 us
    ppermute x2, starting transfers between devices, shift(): lax.ppermute(array, 'tp', [(i, (i + step) % shards) for i in range(shards)])  3.32 us
  transfers between devices with their start and end apart: 17, of which 5 were waited for; matrix products, arithmetic and copies ran while one was open for 2% of the time, Pallas kernels for 54%

profile of v1, /device:TPU:5, one launch (start us, length us, event | category | flops | bytes accessed | tf_op | source)
XLA Modules:
  0.0 136.9 jit_solution(7756667136601391154)
XLA Ops:
  7.9 0.8 concatenate.12
  8.6 5.5 %all-gather.1 = s32[4,1,128]{2,1,0:T(1,128)} all-gather(s32[1,1,128]{2,1,0:T(1,128)S(1)} %pad_bitcast_fusion), channel_id=2, replica_groups=mesh['groups'=2,'inst'=4,'tp'=4] {'inst'}, dimensions={0}, use_global_device_ids=true | all-gather | bytes 2560 | tf_op jit(solution)/shard_map/all_gather | solution.py:495
  14.1 1.1 constant_dynamic-slice_fusion
  15.3 0.9 pad_maximum_fusion
  16.5 1.6 %collective-permute-start.1 = (bf16[256,2048]{1,0:T(8,128)(2,1)}, bf16[256,2048]{1,0:T(8,128)(2,1)}, u32[]{:S(2)}, u32[]{:S(2)}) collective-permute-start(bf16[256,2048]{1,0:T(8,128)(2,1)} %q_ref.1), channel_id=1, source_target_pairs={{0,8},{4,12},{8,0},{12,4},{1,9},{5,13},{9,1},{13,5},{2,10},{6,14},... | collective-permute-start | bytes 3145736 | tf_op jit(solution)/shard_map/ppermute | solution.py:479
  18.1 1.3 collective-permute-start.2
  19.4 2.0 %collective-permute-start.3 = (bf16[256,1280]{1,0:T(8,128)(2,1)S(1)}, bf16[256,1280]{1,0:T(8,128)(2,1)}, u32[]{:S(2)}, u32[]{:S(2)}) collective-permute-start(bf16[256,1280]{1,0:T(8,128)(2,1)S(1)} %copy-done.1), channel_id=1, source_target_pairs={{0,3},{1,0},{2,1},{3,2},{4,7},{5,4},{6,5},{7,6},{8,11},{9,8},{10,9... | collective-permute-start | bytes 1966088 | tf_op jit(solution)/shard_map/ppermute | solution.py:482
  21.5 23.1 %shard_map.122 = (f32[1,9,256,128]{3,2,1,0:T(8,128)}, f32[1,9,256,128]{3,2,1,0:T(8,128)}, f32[1,9,256,128]{3,2,1,0:T(8,128)}, f32[1,9,256,128]{3,2,1,0:T(8,128)}, bf16[2,54,128,256]{3,2,1,0:T(8,128)(2,1)}) custom-call(s32[1]{0:T(128)} %bitcast.refs_0_.me_ref, s32[4,128]{1,0:T(4,128)} %bitcast.11, bf16[256,2048]{1,0:T(8,128)(2,1)} %q_ref.1, ...), custom_call_target="tpu_custom_call" | custom-call | flops 22000001024 | bytes 66000000 | tf_op jit(solution)/shard_map/pallas_call | solution.py:286
  44.6 5.0 %collective-permute-done.3.refs_3_ = bf16[256,1280]{1,0:T(8,128)(2,1)} collective-permute-done((bf16[256,1280]{1,0:T(8,128)(2,1)S(1)}, bf16[256,1280]{1,0:T(8,128)(2,1)}, u32[]{:S(2)}, u32[]{:S(2)}) %collective-permute-start.3) | collective-permute-done | bytes 655392 | tf_op jit(solution)/shard_map/ppermute | solution.py:482
  49.6 1.1 collective-permute-start.4
  50.7 0.7 collective-permute-start.5
  51.4 1.3 collective-permute-start.6
  52.7 0.7 collective-permute-done.4.refs_2_
  53.5 19.6 %shard_map.123 = (f32[1,9,256,128]{3,2,1,0:T(8,128)}, f32[1,9,256,128]{3,2,1,0:T(8,128)}) custom-call(s32[1]{0:T(128)} %bitcast.refs_0_.me_ref, s32[4,128]{1,0:T(4,128)} %bitcast.12, bf16[256,2048]{1,0:T(8,128)(2,1)} %collective-permute-done.4.refs_2_, bf16[2,54,128,256]{3,2,1,0:T(8,128)(2,1)} %refs_4_.5), custom_call_target="tpu_custom_call" | custom-call | flops 12000000000 | bytes 36000000 | tf_op jit(solution)/shard_map/pallas_call | solution.py:286
  73.1 0.9 collective-permute-start.9
  74.7 0.8 pad_maximum_fusion.1
  76.1 2.0 %broadcast_select_fusion.refs_2_ = bf16[256,1280]{1,0:T(8,128)(2,1)} fusion(bf16[256,1280]{1,0:T(8,128)(2,1)S(1)} %collective-permute-done.5, bf16[256,1280]{1,0:T(8,128)(2,1)} %collective-permute-done.6, pred[]{:T(512)S(6)} %ge.3), kind=kLoop, calls=%fused_computation.1 | loop fusion | flops 327680 | bytes 1966081 | tf_op jit(solution)/shard_map/jit(_where)/select_n | solution.py:531
  78.0 6.9 %shard_map.124.fresh_ref.refs_0_ = bf16[2,256,256]{2,1,0:T(8,128)(2,1)} custom-call(s32[1]{0:T(128)} %bitcast.7.rank_ref, f32[256,128]{1,0:T(8,128)} %get-tuple-element.51.cos_ref, f32[256,128]{1,0:T(8,128)} %get-tuple-element.52.sin_ref, f32[1,128]{1,0:T(1,128)} %bitcast.16, bf16[256,1280]{1,0:T(8,128)(2,1)} %refs_0_, ...), custom_call_target="tpu_custom_call" | custom-call | flops 200000000 | bytes 600000 | tf_op jit(solution)/shard_map/pallas_call | solution.py:342
  85.3 8.7 %shard_map.125 = bf16[1,9,256,128]{3,2,1,0:T(8,128)(2,1)} custom-call(s32[1]{0:T(128)} %bitcast.refs_0_.me_ref, s32[4,128]{1,0:T(4,128)} %bitcast.13, bf16[256,2048]{1,0:T(8,128)(2,1)} %collective-permute-done.1.refs_2_, f32[1,9,256,128]{3,2,1,0:T(8,128)} %collective-permute-done.7.refs_3_, bf16[2,54,128,256]{3,2,1,0:T(8,128)(2,1)} %refs_4_.5), custom_call_target="tpu_custom_call" | custom-call | flops 200000000 | bytes 600000 | tf_op jit(solution)/shard_map/pallas_call | solution.py:286
  94.0 4.6 %collective-permute-start.13 = (bf16[1,9,256,128]{3,2,1,0:T(8,128)(2,1)}, bf16[1,9,256,128]{3,2,1,0:T(8,128)(2,1)}, u32[]{:S(2)}, u32[]{:S(2)}) collective-permute-start(bf16[1,9,256,128]{3,2,1,0:T(8,128)(2,1)} %shard_map.125), channel_id=1, source_target_pairs={{0,8},{4,12},{8,0},{12,4},{1,9},{5,13},{9,1},{13,5},{2,10},{6,14},... | collective-permute-start | bytes 1769480 | tf_op jit(solution)/shard_map/ppermute | solution.py:479
  98.6 0.7 copy-done.3
  99.3 8.5 %shard_map.126 = bf16[1,9,256,128]{3,2,1,0:T(8,128)(2,1)} custom-call(s32[1]{0:T(128)} %bitcast.refs_0_.me_ref, s32[4,128]{1,0:T(4,128)} %bitcast.14, bf16[256,2048]{1,0:T(8,128)(2,1)} %collective-permute-done.1.refs_2_, f32[1,9,256,128]{3,2,1,0:T(8,128)} %collective-permute-done.9.refs_3_, bf16[2,54,128,256]{3,2,1,0:T(8,128)(2,1)} %refs_4_.5), custom_call_target="tpu_custom_call" | custom-call | flops 200000000 | bytes 600000 | tf_op jit(solution)/shard_map/pallas_call | solution.py:286
  107.9 3.3 %collective-permute-start.11 = (bf16[1,9,256,128]{3,2,1,0:T(8,128)(2,1)}, bf16[1,9,256,128]{3,2,1,0:T(8,128)(2,1)S(1)}, u32[]{:S(2)}, u32[]{:S(2)}) collective-permute-start(bf16[1,9,256,128]{3,2,1,0:T(8,128)(2,1)} %shard_map.126), channel_id=1, source_target_pairs={{0,8},{4,12},{8,0},{12,4},{1,9},{5,13},{9,1},{13,5},{2,10},{6,14},... | collective-permute-start | bytes 1769480 | tf_op jit(solution)/shard_map/ppermute | solution.py:479
  111.2 1.0 collective-permute-start.14
  112.2 1.2 collective-permute-done.14.refs_1_
  114.4 1.4 %collective-permute-done.15.refs_3_ = bf16[2,256,256]{2,1,0:T(8,128)(2,1)S(1)} collective-permute-done((bf16[2,256,256]{2,1,0:T(8,128)(2,1)}, bf16[2,256,256]{2,1,0:T(8,128)(2,1)S(1)}, u32[]{:S(2)}, u32[]{:S(2)}) %collective-permute-start.15) | collective-permute-done | bytes 262176 | tf_op jit(solution)/shard_map/ppermute | solution.py:479
  115.8 0.7 copy-done.5
  116.5 2.0 %shard_map.129 = bf16[2,54,128,256]{3,2,1,0:T(8,128)(2,1)} custom-call(s32[1]{0:T(128)} %bitcast.refs_0_.me_ref, s32[4,128]{1,0:T(4,128)} %bitcast.15, bf16[2,256,256]{2,1,0:T(8,128)(2,1)} %shard_map.124.fresh_ref.refs_0_, bf16[2,256,256]{2,1,0:T(8,128)(2,1)} %copy-done.4, bf16[2,256,256]{2,1,0:T(8,128)(2,1)} %copy-done.3, ...), custom_call_target="tpu_custom_call", output_to_operand_aliasing={{}: (6, {})} | custom-call | flops 200000000 | bytes 600000 | tf_op jit(solution)/shard_map/pallas_call | solution.py:438
  118.5 4.7 %shard_map.127.refs_3_ = bf16[256,2048]{1,0:T(8,128)(2,1)} custom-call(bf16[256,2048]{1,0:T(8,128)(2,1)} %q_ref.1, bf16[2,256,256]{2,1,0:T(8,128)(2,1)} %shard_map.124.fresh_ref.refs_0_, f32[1,9,256,128]{3,2,1,0:T(8,128)} %get-tuple-element.43.refs_0_, f32[1,9,256,128]{3,2,1,0:T(8,128)} %collective-permute-done.12.refs_1_, ...), custom_call_target="tpu_custom_call" | custom-call | flops 200000000 | bytes 600000 | tf_op jit(solution)/shard_map/pallas_call | solution.py:396
  123.3 1.2 collective-permute-done.11.refs_2_
  124.5 0.8 copy-done.2
  125.3 4.7 %shard_map.128 = bf16[256,2048]{1,0:T(8,128)(2,1)} custom-call(bf16[256,2048]{1,0:T(8,128)(2,1)} %q_ref.1, bf16[2,256,256]{2,1,0:T(8,128)(2,1)} %shard_map.124.fresh_ref.refs_0_, f32[1,9,256,128]{3,2,1,0:T(8,128)} %get-tuple-element.41.refs_0_, f32[1,9,256,128]{3,2,1,0:T(8,128)} %collective-permute-done.10.refs_1_, ...), custom_call_target="tpu_custom_call", output_to_operand_aliasing={{}: (5, {})} | custom-call | flops 200000000 | bytes 600000 | tf_op jit(solution)/shard_map/pallas_call | solution.py:396
  (33 shorter events, 2.9 us)
Async XLA Ops:
  7.2 70.9 %all-gather.4.cloned.1.call-start = ((), (), s32[]{:S(2)}) async-start(), calls=%async_computation | async-start | bytes 5898240 | tf_op jit(solution)/shard_map/all_gather | solution.py:511
  15.3 2.9 %copy-start.1 = (bf16[256,1280]{1,0:T(8,128)(2,1)S(1)}, bf16[256,1280]{1,0:T(8,128)(2,1)}, u32[]{:S(2)}) copy-start(bf16[256,1280]{1,0:T(8,128)(2,1)} %refs_0_) | copy-start | bytes 1966084
  16.2 5.3 %collective-permute-start = (bf16[256,2048]{1,0:T(8,128)(2,1)}, bf16[256,2048]{1,0:T(8,128)(2,1)}, u32[]{:S(2)}, u32[]{:S(2)}) collective-permute-start(bf16[256,2048]{1,0:T(8,128)(2,1)} %q_ref.1), channel_id=1, source_target_pairs={{0,4},{4,0},{8,12},{12,8},{1,5},{5,1},{9,13},{13,9},{2,6},{6,2},{1... | collective-permute-start | bytes 3145736 | tf_op jit(solution)/shard_map/ppermute | solution.py:479
  16.5 33.1 %collective-permute-start.1 = (bf16[256,2048]{1,0:T(8,128)(2,1)}, bf16[256,2048]{1,0:T(8,128)(2,1)}, u32[]{:S(2)}, u32[]{:S(2)}) collective-permute-start(bf16[256,2048]{1,0:T(8,128)(2,1)} %q_ref.1), channel_id=1, source_target_pairs={{0,8},{4,12},{8,0},{12,4},{1,9},{5,13},{9,1},{13,5},{2,10},{6,14},... | collective-permute-start | bytes 3145736 | tf_op jit(solution)/shard_map/ppermute | solution.py:479
  18.1 26.5 %collective-permute-start.2 = (bf16[256,1280]{1,0:T(8,128)(2,1)S(1)}, bf16[256,1280]{1,0:T(8,128)(2,1)}, u32[]{:S(2)}, u32[]{:S(2)}) collective-permute-start(bf16[256,1280]{1,0:T(8,128)(2,1)S(1)} %copy-done.1), channel_id=1, source_target_pairs={{0,1},{1,2},{2,3},{3,0},{4,5},{5,6},{6,7},{7,4},{8,9},{9,10},{10,1... | collective-permute-start | bytes 1966088 | tf_op jit(solution)/shard_map/ppermute | solution.py:482
  19.4 30.2 %collective-permute-start.3 = (bf16[256,1280]{1,0:T(8,128)(2,1)S(1)}, bf16[256,1280]{1,0:T(8,128)(2,1)}, u32[]{:S(2)}, u32[]{:S(2)}) collective-permute-start(bf16[256,1280]{1,0:T(8,128)(2,1)S(1)} %copy-done.1), channel_id=1, source_target_pairs={{0,3},{1,0},{2,1},{3,2},{4,7},{5,4},{6,5},{7,6},{8,11},{9,8},{10,9... | collective-permute-start | bytes 1966088 | tf_op jit(solution)/shard_map/ppermute | solution.py:482
  49.6 3.8 %collective-permute-start.4 = (bf16[256,2048]{1,0:T(8,128)(2,1)}, bf16[256,2048]{1,0:T(8,128)(2,1)}, u32[]{:S(2)}, u32[]{:S(2)}) collective-permute-start(bf16[256,2048]{1,0:T(8,128)(2,1)} %collective-permute-done.1.refs_2_), channel_id=1, source_target_pairs={{0,4},{4,0},{8,12},{12,8},{1,5},{5,1},{9,13},{13,9},{2,6},{6,2},{1... | collective-permute-start | bytes 3145736 | tf_op jit(solution)/shard_map/ppermute | solution.py:479
  50.7 22.4 %collective-permute-start.5 = (bf16[256,1280]{1,0:T(8,128)(2,1)}, bf16[256,1280]{1,0:T(8,128)(2,1)S(1)}, u32[]{:S(2)}, u32[]{:S(2)}) collective-permute-start(bf16[256,1280]{1,0:T(8,128)(2,1)} %collective-permute-done.2.refs_1_), channel_id=1, source_target_pairs={{1,2},{2,3},{5,6},{6,7},{9,10},{10,11},{13,14},{14,15},{17,18},{18... | collective-permute-start | bytes 1966088 | tf_op jit(solution)/shard_map/ppermute | solution.py:529
  51.4 21.7 %collective-permute-start.6 = (bf16[256,1280]{1,0:T(8,128)(2,1)}, bf16[256,1280]{1,0:T(8,128)(2,1)}, u32[]{:S(2)}, u32[]{:S(2)}) collective-permute-start(bf16[256,1280]{1,0:T(8,128)(2,1)} %collective-permute-done.3.refs_3_), channel_id=1, source_target_pairs={{1,0},{2,1},{5,4},{6,5},{9,8},{10,9},{13,12},{14,13},{17,16},{18,1... | collective-permute-start | bytes 1966088 | tf_op jit(solution)/shard_map/ppermute | solution.py:530
  73.1 25.5 %collective-permute-start.9 = (f32[1,9,256,128]{3,2,1,0:T(8,128)}, f32[1,9,256,128]{3,2,1,0:T(8,128)}, u32[]{:S(2)}, u32[]{:S(2)}) collective-permute-start(f32[1,9,256,128]{3,2,1,0:T(8,128)} %get-tuple-element.39), channel_id=1, source_target_pairs={{0,4},{4,0},{8,12},{12,8},{1,5},{5,1},{9,13},{13,9},{2,6},{6,2},{1... | collective-permute-start | bytes 3538952 | tf_op jit(solution)/shard_map/ppermute | solution.py:479
  74.1 11.2 %collective-permute-start.7 = (f32[1,9,256,128]{3,2,1,0:T(8,128)}, f32[1,9,256,128]{3,2,1,0:T(8,128)}, u32[]{:S(2)}, u32[]{:S(2)}) collective-permute-start(f32[1,9,256,128]{3,2,1,0:T(8,128)} %get-tuple-element.37), channel_id=1, source_target_pairs={{0,4},{4,0},{8,12},{12,8},{1,5},{5,1},{9,13},{13,9},{2,6},{6,2},{1... | collective-permute-start | bytes 3538952 | tf_op jit(solution)/shard_map/ppermute | solution.py:479
  75.5 43.0 %collective-permute-start.12 = (f32[1,9,256,128]{3,2,1,0:T(8,128)}, f32[1,9,256,128]{3,2,1,0:T(8,128)}, u32[]{:S(2)}, u32[]{:S(2)}) collective-permute-start(f32[1,9,256,128]{3,2,1,0:T(8,128)} %get-tuple-element.45), channel_id=1, source_target_pairs={{0,4},{4,0},{8,12},{12,8},{1,5},{5,1},{9,13},{13,9},{2,6},{6,2},{1... | collective-permute-start | bytes 3538952 | tf_op jit(solution)/shard_map/ppermute | solution.py:479
  76.0 47.3 %collective-permute-start.10 = (f32[1,9,256,128]{3,2,1,0:T(8,128)}, f32[1,9,256,128]{3,2,1,0:T(8,128)}, u32[]{:S(2)}, u32[]{:S(2)}) collective-permute-start(f32[1,9,256,128]{3,2,1,0:T(8,128)} %get-tuple-element.42), channel_id=1, source_target_pairs={{0,4},{4,0},{8,12},{12,8},{1,5},{5,1},{9,13},{13,9},{2,6},{6,2},{1... | collective-permute-start | bytes 3538952 | tf_op jit(solution)/shard_map/ppermute | solution.py:479
  85.0 13.6 %collective-permute-start.8 = (bf16[2,256,256]{2,1,0:T(8,128)(2,1)}, bf16[2,256,256]{2,1,0:T(8,128)(2,1)S(1)}, u32[]{:S(2)}, u32[]{:S(2)}) collective-permute-start(bf16[2,256,256]{2,1,0:T(8,128)(2,1)} %shard_map.124.fresh_ref.refs_0_), channel_id=1, source_target_pairs={{0,8},{4,12},{8,0},{12,4},{1,9},{5,13},{9,1},{13,5},{2,10},{6,14},... | collective-permute-start | bytes 786440 | tf_op jit(solution)/shard_map/ppermute | solution.py:479
  94.0 17.2 %copy-start = (bf16[2,256,256]{2,1,0:T(8,128)(2,1)S(1)}, bf16[2,256,256]{2,1,0:T(8,128)(2,1)}, u32[]{:S(2)}) copy-start(bf16[2,256,256]{2,1,0:T(8,128)(2,1)} %shard_map.124.fresh_ref.refs_0_) | copy-start | bytes 786436
  94.0 24.5 %collective-permute-start.13 = (bf16[1,9,256,128]{3,2,1,0:T(8,128)(2,1)}, bf16[1,9,256,128]{3,2,1,0:T(8,128)(2,1)}, u32[]{:S(2)}, u32[]{:S(2)}) collective-permute-start(bf16[1,9,256,128]{3,2,1,0:T(8,128)(2,1)} %shard_map.125), channel_id=1, source_target_pairs={{0,8},{4,12},{8,0},{12,4},{1,9},{5,13},{9,1},{13,5},{2,10},{6,14},... | collective-permute-start | bytes 1769480 | tf_op jit(solution)/shard_map/ppermute | solution.py:479
  98.6 0.7 copy-start.3
  107.9 16.6 %collective-permute-start.11 = (bf16[1,9,256,128]{3,2,1,0:T(8,128)(2,1)}, bf16[1,9,256,128]{3,2,1,0:T(8,128)(2,1)S(1)}, u32[]{:S(2)}, u32[]{:S(2)}) collective-permute-start(bf16[1,9,256,128]{3,2,1,0:T(8,128)(2,1)} %shard_map.126), channel_id=1, source_target_pairs={{0,8},{4,12},{8,0},{12,4},{1,9},{5,13},{9,1},{13,5},{2,10},{6,14},... | collective-permute-start | bytes 1769480 | tf_op jit(solution)/shard_map/ppermute | solution.py:479
  111.2 2.1 %collective-permute-start.14 = (bf16[2,256,256]{2,1,0:T(8,128)(2,1)S(1)}, bf16[2,256,256]{2,1,0:T(8,128)(2,1)S(1)}, u32[]{:S(2)}, u32[]{:S(2)}) collective-permute-start(bf16[2,256,256]{2,1,0:T(8,128)(2,1)S(1)} %copy-done), channel_id=1, source_target_pairs={{0,4},{4,0},{8,12},{12,8},{1,5},{5,1},{9,13},{13,9},{2,6},{6,2},{1... | collective-permute-start | bytes 786440 | tf_op jit(solution)/shard_map/ppermute | solution.py:479
  113.4 0.7 copy-start.4
  114.1 1.7 %collective-permute-start.15 = (bf16[2,256,256]{2,1,0:T(8,128)(2,1)}, bf16[2,256,256]{2,1,0:T(8,128)(2,1)S(1)}, u32[]{:S(2)}, u32[]{:S(2)}) collective-permute-start(bf16[2,256,256]{2,1,0:T(8,128)(2,1)} %copy-done.3), channel_id=1, source_target_pairs={{0,4},{4,0},{8,12},{12,8},{1,5},{5,1},{9,13},{13,9},{2,6},{6,2},{1... | collective-permute-start | bytes 786440 | tf_op jit(solution)/shard_map/ppermute | solution.py:479
  115.8 0.7 copy-start.5
  124.5 0.8 copy-start.2
Sparse Core Ops, SparseCore 0:
  16.3 49.3 all-gather.3
